TPU v7x, 32 devices: a whole 2x2x4 slice. The times are simulated.
32 devices in a mesh: groups: 2 (over x), dp: 2 (over core), expert: 8 (over z, y).
Axes of the slice: x: 2, y: 2, z: 4, core: 2. Of those that a mesh axis runs over, the one named last changes fastest.
Arguments:
- tokens: bfloat16 [1024, 7168], P(('groups', 'dp', 'expert')), parts along dimension 0, may hold values from -6 to 6
- routes: int32 [1024, 4], P(('groups', 'dp', 'expert')), parts along dimension 0, may hold values from 0 to 7, all different within a row; in each aligned block of 32 rows (0 to 31, 32 to 63, ...) at most 32 rows name the same one
- gate_weights: float32 [1024, 4], P(('groups', 'dp', 'expert')), parts along dimension 0, may hold values from 0.05 to 0.6
- w_gate: bfloat16 [8, 7168, 1024], P('expert', None, 'dp'), may hold values from -0.0625 to 0.0625
- w_up: bfloat16 [8, 7168, 1024], P('expert', None, 'dp'), may hold values from -0.0625 to 0.0625
- w_down: bfloat16 [8, 1024, 7168], P('expert', 'dp'), may hold values from -0.1875 to 0.1875
Outputs:
- layer_out: bfloat16 [1024, 7168], P(('groups', 'dp', 'expert')), parts along dimension 0
There are 2 independent parts, one for each index of `groups`. A program takes and returns all parts, laid end to end along the dimension named above; an argument that names none is the same for every part. Nothing has to cross between parts.
Inputs may be any that keep to these rules, and one draw needn't show every extreme that they name: `routes`: each row names 4 different experts. Among the rows of one device (aligned blocks of 32 rows) no expert is named more than 32 times, a bound that some block reaches.
All inputs are finite; a program needn't handle non-finite values.
Results may differ from a plain program's by a relative error of at most 0.0085.
Values may be sent and summed in bfloat16 or wider, within the bound.
A program may use at most 128 MiB of HBM per device.

v0:
```python
import jax
import jax.numpy as jnp
from jax import lax
from jax.sharding import PartitionSpec as P


def local(tokens, routes, gate_weights, w_gate, w_up, w_down):
    tok_count, model_width = tokens.shape
    top_count = routes.shape[1]
    experts = lax.axis_size("expert")
    capacity = 2 * tok_count * top_count // experts
    flat_exp = routes.reshape(-1)
    flat_tok = jnp.arange(tok_count * top_count, dtype=jnp.int32) // top_count
    onehot = (flat_exp[:, None] == jnp.arange(experts, dtype=jnp.int32)[None, :]).astype(jnp.int32)
    before = jnp.cumsum(onehot, axis=0) - onehot
    position = jnp.sum(before * onehot, axis=1)
    slot_index = flat_exp * capacity + position
    source = jnp.full((experts * capacity,), tok_count, jnp.int32).at[slot_index].set(flat_tok)
    padded = jnp.concatenate([tokens, jnp.zeros((1, model_width), jnp.bfloat16)], 0)
    outgoing = padded[source].reshape(experts, capacity, model_width)
    arrived = lax.all_to_all(outgoing, "expert", split_axis=0, concat_axis=0, tiled=True)
    row_data = lax.all_gather(arrived, "dp", axis=0, tiled=True).reshape(-1, model_width)
    gate_out = jnp.dot(row_data, w_gate[0], preferred_element_type=jnp.float32)
    up_out = jnp.dot(row_data, w_up[0], preferred_element_type=jnp.float32)
    hidden = (jax.nn.silu(gate_out) * up_out).astype(jnp.bfloat16)
    summed = lax.psum_scatter(
        jnp.dot(hidden, w_down[0], preferred_element_type=jnp.float32).astype(jnp.bfloat16),
        "dp",
        scatter_dimension=0,
        tiled=True,
    ).astype(jnp.float32)
    returned = lax.all_to_all(
        summed.reshape(experts, capacity, model_width).astype(jnp.bfloat16),
        "expert",
        split_axis=0,
        concat_axis=0,
        tiled=True,
    ).astype(jnp.float32)
    per_slot = returned.reshape(experts * capacity, model_width)
    gathered = per_slot[slot_index].reshape(tok_count, top_count, model_width)
    layer_out = jnp.sum(gathered * gate_weights[:, :, None], axis=1)
    return layer_out.astype(jnp.bfloat16)


def solution(mesh):
    return jax.shard_map(
        local,
        mesh=mesh,
        in_specs=(
            P(("groups", "dp", "expert"), None),
            P(("groups", "dp", "expert"), None),
            P(("groups", "dp", "expert"), None),
            P("expert", None, "dp"),
            P("expert", None, "dp"),
            P("expert", "dp", None),
        ),
        out_specs=P(("groups", "dp", "expert"), None),
        check_vma=False,
    )
```

profile of v0, /device:TPU:0, one launch (start us, length us, event | category | flops | bytes accessed | tf_op | source)
XLA Modules:
  0.0 285.2 jit_solution(5018690452848221197)
XLA Ops:
  6.5 0.0 all-gather.2.cloned.1.call-start
  6.5 0.8 copy.14
  7.3 0.7 broadcast_multiply_fusion
  8.0 0.1 eq.15
  8.1 0.1 fusion.11
  8.2 0.2 reduce_window_sum.11
  8.4 0.2 select_reduce_fusion
  8.5 0.1 copy.13
  8.6 0.1 mul.36
  8.8 1.0 scatter_custom_fusion
  9.8 1.1 concatenate.3
  10.8 4.7 %gather_fusion = bf16[256,7168]{1,0:T(8,128)(2,1)} fusion(bf16[33,7168]{1,0:T(8,128)(2,1)S(1)} %concatenate.3, s32[1024]{0:T(1024)S(1)} %pad_clamp_fusion.1), kind=kCustom, calls=%fused_computation | custom fusion | bytes 7341056 | tf_op jit(solution)/shard_map/gather | solution.py:20
  15.5 89.3 %all_to_all.10 = bf16[8,32,7168]{2,1,0:T(8,128)(2,1)} all-to-all(bf16[8,32,7168]{2,1,0:T(8,128)(2,1)} %bitcast.28), channel_id=1, replica_groups=mesh['groups'=2,'dp'=2,'expert'=8] {'expert'}, dimensions={0} | all-to-all | bytes 7340032 | tf_op jit(solution)/shard_map/all_to_all | solution.py:21
  104.9 0.0 all-gather.2.cloned.1.call-update
  104.9 0.0 reduce-scatter.2.cloned.1.call-start
  104.9 17.4 %all-gather.2.cloned.1.call-done = bf16[16,32,7168]{2,1,0:T(8,128)(2,1)} async-done(((bf16[8,32,7168]{2,1,0:T(8,128)(2,1)}), bf16[16,32,7168]{2,1,0:T(8,128)(2,1)}) %all-gather.2.cloned.1.call-update) | async-done | bytes 7340048 | tf_op jit(solution)/shard_map/all_gather | solution.py:22
  122.3 0.0 copy-start.1
  122.3 9.5 %fusion.3 = f32[512,512]{1,0:T(8,128)S(1)} fusion(bf16[512,7168]{1,0:T(8,128)(2,1)} %bitcast.30, bf16[1,7168,512]{2,1,0:T(8,128)(2,1)} %param.9), kind=kOutput, calls=%fused_computation.7 | convolution fusion | flops 3758096384 | bytes 15728640 | tf_op jit(solution)/shard_map/dot_general | solution.py:23
  131.8 0.0 copy-done.1
  131.8 7.2 %fusion.8 = bf16[512,512]{1,0:T(8,128)(2,1)S(1)} fusion(bf16[512,7168]{1,0:T(8,128)(2,1)S(1)} %bitcast.31, bf16[1,7168,512]{2,1,0:T(8,128)(2,1)} %param.10, f32[512,512]{1,0:T(8,128)S(1)} %fusion.3), kind=kOutput, calls=%fused_computation.12 | convolution fusion | flops 3759669248 | bytes 16252928 | tf_op jit(solution)/shard_map/dot_general | solution.py:24
  139.0 9.4 %convolution_convert_fusion = bf16[512,7168]{1,0:T(8,128)(2,1)} fusion(bf16[512,512]{1,0:T(8,128)(2,1)S(1)} %fusion.8, bf16[1,512,7168]{2,1,0:T(8,128)(2,1)} %param.11), kind=kOutput, calls=%fused_computation.3 | convolution fusion | flops 3761766400 | bytes 15204352 | tf_op jit(solution)/shard_map/dot_general | solution.py:27
  148.4 0.0 copy-start
  148.4 0.0 reduce-scatter.2.cloned.1.call-update
  148.4 17.2 %reduce-scatter.2.cloned.1.call-done = bf16[256,7168]{1,0:T(8,128)(2,1)} async-done(((bf16[512,7168]{1,0:T(8,128)(2,1)}), bf16[256,7168]{1,0:T(8,128)(2,1)}) %reduce-scatter.2.cloned.1.call-update) | async-done | bytes 3670032 | tf_op jit(solution)/shard_map/reduce_scatter | solution.py:26
  165.6 5.7 %all-to-all-start.1 = ((bf16[8,32,7168]{2,1,0:T(8,128)(2,1)}), bf16[8,32,7168]{2,1,0:T(8,128)(2,1)}, u32[]{:S(2)}, u32[]{:S(2)}) async-start(bf16[8,32,7168]{2,1,0:T(8,128)(2,1)} %bitcast.29), calls=%async_computation.2 | async-start | bytes 7340032 | tf_op jit(solution)/shard_map/all_to_all | solution.py:32
  171.4 0.0 copy-done
  171.4 0.1 copy.15
  171.5 82.4 %all-to-all-done.1 = bf16[8,32,7168]{2,1,0:T(8,128)(2,1)} async-done(((bf16[8,32,7168]{2,1,0:T(8,128)(2,1)}), bf16[8,32,7168]{2,1,0:T(8,128)(2,1)}, u32[]{:S(2)}, u32[]{:S(2)}) %all-to-all-start.1) | async-done | bytes 3670048 | tf_op jit(solution)/shard_map/all_to_all | solution.py:32
  253.9 5.9 %bitcast_convert_fusion = f32[256,7168]{1,0:T(8,128)} fusion(bf16[8,32,7168]{2,1,0:T(8,128)(2,1)} %all-to-all-done.1), kind=kLoop, calls=%fused_computation.9 | loop fusion | flops 1835008 | bytes 11010048 | tf_op jit(solution)/shard_map/reshape | solution.py:39
  259.8 8.2 %gather_fusion.1 = f32[128,7168]{1,0:T(8,128)} fusion(f32[256,7168]{1,0:T(8,128)} %bitcast_convert_fusion, s32[1024]{0:T(1024)S(1)} %pad_clamp_fusion), kind=kCustom, calls=%fused_computation.1 | custom fusion | bytes 7340544 | tf_op jit(solution)/shard_map/gather | solution.py:40
  267.9 5.2 %reshape.52 = f32[32,4,7168]{2,1,0:T(4,128)} reshape(f32[128,7168]{1,0:T(8,128)} %gather_fusion.1) | data formatting | bytes 7340032 | tf_op jit(solution)/shard_map/reshape | solution.py:40
  273.1 5.3 %multiply_reduce_fusion = bf16[32,7168]{1,0:T(8,128)(2,1)} fusion(f32[32,4,7168]{2,1,0:T(4,128)} %reshape.52, f32[32,4]{1,0:T(8,128)S(1)} %copy.15), kind=kLoop, calls=%fused_computation.10 | loop fusion | flops 1605632 | bytes 4129280 | tf_op jit(solution)/shard_map/reduce_sum | solution.py:41
  (5 shorter events, 0.0 us)
Async XLA Ops:
  6.5 115.8 %all-gather.2.cloned.1.call-start = ((), (), s32[]{:S(2)}) async-start(), calls=%async_computation.3 | async-start | bytes 11010048 | tf_op jit(solution)/shard_map/all_gather | solution.py:22
  104.9 60.7 %reduce-scatter.2.cloned.1.call-start = ((), (), s32[]{:S(2)}) async-start(), calls=%async_computation.4 | async-start | bytes 11010048 | tf_op jit(solution)/shard_map/reduce_scatter | solution.py:26
  122.3 9.5 %copy-start.1 = (bf16[16,32,7168]{2,1,0:T(8,128)(2,1)S(1)}, bf16[16,32,7168]{2,1,0:T(8,128)(2,1)}, u32[]{:S(2)}) copy-start(bf16[16,32,7168]{2,1,0:T(8,128)(2,1)} %all-gather.2.cloned.1.call-done) | copy-start | bytes 22020100
  148.4 23.0 %copy-start = (f32[32,4]{0,1:T(4,128)S(1)}, f32[32,4]{0,1:T(4,128)}, u32[]{:S(2)}) copy-start(f32[32,4]{0,1:T(4,128)} %param.8) | copy-start | bytes 1540
  165.6 88.3 %all-to-all-start.1 = ((bf16[8,32,7168]{2,1,0:T(8,128)(2,1)}), bf16[8,32,7168]{2,1,0:T(8,128)(2,1)}, u32[]{:S(2)}, u32[]{:S(2)}) async-start(bf16[8,32,7168]{2,1,0:T(8,128)(2,1)} %bitcast.29), calls=%async_computation.2 | async-start | bytes 7340032 | tf_op jit(solution)/shard_map/all_to_all | solution.py:32
Sparse Core Ops, SparseCore 0:
  105.0 17.3 all-gather.1
  148.5 17.0 reduce-scatter.1
where the time goes:
time: 286 us; the launch traced here: 285 us
  waiting for transfers between devices  117 us (41%)
  blocking collectives  89.3 us (31%)
  matrix products  26 us (9%)
  local copies, waits for them, and re-layouts  21.2 us (7%)
  between operations  13.5 us (5%)
  other arithmetic  12.3 us (4%)
  starting transfers between devices  5.79 us (2%)
    all_to_all x1, blocking collectives, local(): lax.all_to_all(outgoing, 'expert', split_axis=0, concat_axis=0, tiled=True)  89.3 us
    all_to_all x1, waiting for transfers between devices, local(): lax.all_to_all(summed.reshape(experts, capacity, model_width).astype(jnp....  82.4 us
    all_gather x1, waiting for transfers between devices, local(): lax.all_gather(arrived, 'dp', axis=0, tiled=True).reshape(-1, model_width)  17.4 us
    reduce_scatter x1, waiting for transfers between devices, local(): lax.psum_scatter(jnp.dot(hidden, w_down[0], preferred_element_type=jnp.fl...  17.2 us
    dot_general x1, matrix products, local(): gate_out = jnp.dot(row_data, w_gate[0], preferred_element_type=jnp.float32)  9.48 us
    dot_general x1, matrix products, local(): jnp.dot(hidden, w_down[0], preferred_element_type=jnp.float32)  9.37 us
    gather x1, local copies, waits for them, and re-layouts, local(): gathered = per_slot[slot_index].reshape(tok_count, top_count, model_width)  8.18 us
    dot_general x1, matrix products, local(): up_out = jnp.dot(row_data, w_up[0], preferred_element_type=jnp.float32)  7.17 us
  transfers between devices with their start and end apart: 3, of which 3 were waited for; matrix products, arithmetic and copies ran while one was open for 0% of the time, Pallas kernels for 0%

commit v1 on v0

v1 whole, which is shorter than its diff:
```python
import functools

import jax
import jax.numpy as jnp
from jax import lax
from jax.experimental import pallas as pl
from jax.experimental.pallas import tpu as pltpu
from jax.sharding import PartitionSpec as P

MESH = pl.DeviceIdType.MESH
LANES = 128


def ring_place(n, expert):
    if n != 8:
        return expert
    return lax.select(lax.rem(expert, 2) == 0, expert // 2, (2 * n - 1 - expert) // 2)


def ring_expert(n, place):
    if n != 8:
        return place
    return lax.select(place < n // 2, 2 * place, 2 * n - 1 - 2 * place)


def kernel(n, tokens, routes, gates, w_gate, w_up, w_down, out,
           x, mine, theirs, back, wg, wu, wd, hid,
           w_sem, fwd_send, fwd_recv, pair_send, pair_recv, sum_send, sum_recv, back_send, back_recv):
    rows, width = tokens.shape
    top = routes.shape[1]
    ffd = wg.shape[1]
    half, sub = n // 2, rows // 2
    expert = lax.axis_index("expert")
    core = lax.axis_index("dp")
    place = ring_place(n, expert)
    nxt = ring_expert(n, lax.rem(place + 1, n))
    prv = ring_expert(n, lax.rem(place + n - 1, n))
    ahead, partner = ({"expert": nxt}, {"expert": prv}), {"dp": 1 - core}

    def slot(d, s):
        return 0 if s == 0 else n - 1 if s == half else 2 * s - 1 + d

    def rdma(src, dst, send, recv, device):
        return pltpu.make_async_remote_copy(
            src_ref=src, dst_ref=dst, send_sem=send, recv_sem=recv, device_id=device, device_id_type=MESH)

    loads = [pltpu.make_async_copy(src.at[0], dst, w_sem.at[i])
             for i, (src, dst) in enumerate(((w_gate, wg), (w_up, wu), (w_down, wd)))]
    for load in loads:
        load.start()

    barrier = pltpu.get_barrier_semaphore()
    for device in (*ahead, partner):
        pl.semaphore_signal(barrier, inc=1, device_id=device, device_id_type=MESH)

    x[0:rows, 0:width] = tokens[...]
    lane = lax.broadcasted_iota(jnp.int32, (rows, LANES), 1)
    left = jnp.zeros((rows, LANES), jnp.float32)
    for k in range(top):
        for part in range(3):
            left = left + jnp.where(lane == routes[:, k:k + 1] + part * n, gates[:, k:k + 1], 0.0)
    high = left.astype(jnp.bfloat16).astype(jnp.float32)
    mid = (left - high).astype(jnp.bfloat16).astype(jnp.float32)
    low = left - high - mid
    x[0:rows, width:width + LANES] = jnp.where(lane < n, high, jnp.where(lane < 2 * n, mid, low)).astype(jnp.bfloat16)
    pl.semaphore_wait(barrier, 3)

    def forward(d, s, c):
        a, b = slot(d, s) * 2 * rows + c * sub, slot(d, s + 1) * 2 * rows + c * sub
        return rdma(x.at[pl.ds(a, sub)], x.at[pl.ds(b, sub)],
                    fwd_send.at[d, s, c], fwd_recv.at[d, s + 1, c], ahead[d])

    def pair(b):
        return rdma(x.at[pl.ds(b * 2 * rows, rows)], x.at[pl.ds(b * 2 * rows + rows, rows)],
                    pair_send.at[b], pair_recv.at[b], partner)

    def summed(b):
        return rdma(x.at[pl.ds(b * 2 * rows + rows, rows), pl.ds(0, width)], theirs.at[pl.ds(b * rows, rows)],
                    sum_send.at[b], sum_recv.at[b], partner)

    sent = []

    def start(copy):
        copy.start()
        sent.append(copy)

    def compute(first, blocks):
        base, count = first * 2 * rows, blocks * 2 * rows
        span = pl.ds(base, count)
        tile = min(256, ffd)

        def up(j, _):
            cols = pl.ds(pl.multiple_of(j * tile, tile), tile)
            g = jnp.dot(x[span, 0:width], wg[:, cols], preferred_element_type=jnp.float32)
            u = jnp.dot(x[span, 0:width], wu[:, cols], preferred_element_type=jnp.float32)
            hid[0:count, cols] = (g / (1.0 + jnp.exp(-g)) * u).astype(jnp.bfloat16)
            return 0

        lax.fori_loop(0, ffd // tile, up, 0)
        lane = lax.broadcasted_iota(jnp.int32, (count, LANES), 1)
        own = (lane == expert) | (lane == expert + n) | (lane == expert + 2 * n)
        weight = jnp.sum(jnp.where(own, x[span, width:width + LANES].astype(jnp.float32), 0.0), axis=1, keepdims=True)
        wide = 512 if width % 512 == 0 else LANES

        def down(j, _):
            cols = pl.ds(pl.multiple_of(j * wide, wide), wide)
            y = jnp.dot(hid[0:count, :], wd[:, cols], preferred_element_type=jnp.float32)
            y = (y * weight).astype(jnp.bfloat16)
            for i in range(blocks):
                at = i * 2 * rows
                mine[(first + i) * rows:(first + i + 1) * rows, cols] = y[at:at + rows]
                x[base + at + rows:base + at + 2 * rows, cols] = y[at + rows:at + 2 * rows]
            return 0

        lax.fori_loop(0, width // wide, down, 0)
        for i in range(blocks):
            start(summed(first + i))

    for c in (0, 1):
        for d in (0, 1):
            start(forward(d, 0, c))
    start(pair(0))
    for s in range(1, half):
        for c in (0, 1):
            for d in (0, 1):
                forward(d, s - 1, c).wait_recv()
                if s < half - 1 or c == d:
                    start(forward(d, s, c))
        for d in (0, 1):
            start(pair(slot(d, s)))
        if s == 1:
            for load in loads:
                load.wait()
            pair(0).wait_recv()
            compute(0, 1)
        for d in (0, 1):
            pair(slot(d, s)).wait_recv()
        compute(slot(0, s), 2)

    def home(d, s, c):
        at = slot(1 - d, s) * rows + c * sub
        from_ = mine.at[pl.ds(at, sub)] if s == (half if c != d else half - 1) else back.at[pl.ds((d * half + s) * rows + c * sub, sub)]
        return rdma(from_, back.at[pl.ds((d * half + s - 1) * rows + c * sub, sub)],
                    back_send.at[d, s, c], back_recv.at[d, s - 1, c], ahead[d])

    wide = 1024 if width % 1024 == 0 else LANES

    def step(d, s, c, last):
        at = slot(1 - d, s) * rows + c * sub
        if not last:
            home(d, s + 1, c).wait_recv()
        here = (d * half + s) * rows + c * sub

        def add(j, _):
            cols = pl.ds(pl.multiple_of(j * wide, wide), wide)
            total = mine[at:at + sub, cols].astype(jnp.float32) + theirs[at:at + sub, cols].astype(jnp.float32)
            if last:
                mine[at:at + sub, cols] = total.astype(jnp.bfloat16)
            else:
                total = total + back[here:here + sub, cols].astype(jnp.float32)
                back[here:here + sub, cols] = total.astype(jnp.bfloat16)
            return 0

        lax.fori_loop(0, width // wide, add, 0)
        start(home(d, s, c))

    def finish(c):
        for d in (0, 1):
            home(d, 1, c).wait_recv()
        a, b, t = c * sub, half * rows + c * sub, c * sub

        def add(j, _):
            cols = pl.ds(pl.multiple_of(j * wide, wide), wide)
            total = mine[t:t + sub, cols].astype(jnp.float32) + theirs[t:t + sub, cols].astype(jnp.float32)
            total = total + back[a:a + sub, cols].astype(jnp.float32) + back[b:b + sub, cols].astype(jnp.float32)
            out[t:t + sub, cols] = total.astype(jnp.bfloat16)
            return 0

        lax.fori_loop(0, width // wide, add, 0)

    for b in range(n - 1):
        summed(b).wait_recv()
    for d in (0, 1):
        step(d, half - 1, d, True)
    for d in (0, 1):
        forward(d, half - 1, d).wait_recv()
    start(pair(n - 1))
    pair(n - 1).wait_recv()
    compute(n - 1, 1)
    summed(n - 1).wait_recv()
    for d in (0, 1):
        step(d, half, 1 - d, True)
    for i in range(1, half):
        for d in (0, 1):
            if half - 1 - i > 0:
                step(d, half - 1 - i, d, False)
        for d in (0, 1):
            step(d, half - i, 1 - d, False)
    for c in (0, 1):
        finish(c)
    for copy in sent:
        copy.wait_send()


def local(tokens, routes, gate_weights, w_gate, w_up, w_down):
    rows, width = tokens.shape
    n = lax.axis_size("expert")
    half, ffd = n // 2, w_gate.shape[2]
    bf = jnp.bfloat16
    dma = pltpu.SemaphoreType.DMA
    vmem, anyw = pl.BlockSpec(memory_space=pltpu.VMEM), pl.BlockSpec(memory_space=pl.ANY)
    return pl.pallas_call(
        functools.partial(kernel, n),
        out_shape=jax.ShapeDtypeStruct((rows, width), bf),
        in_specs=[vmem, vmem, vmem, anyw, anyw, anyw],
        out_specs=vmem,
        scratch_shapes=[
            pltpu.VMEM((2 * n * rows, width + LANES), bf),
            pltpu.VMEM((n * rows, width), bf),
            pltpu.VMEM((n * rows, width), bf),
            pltpu.VMEM((n * rows, width), bf),
            pltpu.VMEM((width, ffd), bf),
            pltpu.VMEM((width, ffd), bf),
            pltpu.VMEM((ffd, width), bf),
            pltpu.VMEM((4 * rows, ffd), bf),
            dma((3,)),
            dma((2, half + 1, 2)), dma((2, half + 1, 2)),
            dma((n,)), dma((n,)),
            dma((n,)), dma((n,)),
            dma((2, half + 1, 2)), dma((2, half + 1, 2)),
        ],
        compiler_params=pltpu.CompilerParams(
            collective_id=0, has_side_effects=True, vmem_limit_bytes=61 * 2 ** 20),
        cost_estimate=pl.CostEstimate(
            flops=12 * n * rows * width * ffd, bytes_accessed=6 * width * ffd, transcendentals=2 * n * rows * ffd),
    )(tokens, routes, gate_weights, w_gate, w_up, w_down)


def solution(mesh):
    spread = P(("groups", "dp", "expert"), None)
    return jax.shard_map(
        local,
        mesh=mesh,
        in_specs=(spread, spread, spread, P("expert", None, "dp"), P("expert", None, "dp"), P("expert", "dp", None)),
        out_specs=spread,
        check_vma=False,
    )
```

time: 286 us -> 101 us (0.35)
  waiting for transfers between devices: 117 us -> 0 us
  Pallas kernels: 0 us -> 96.1 us
  blocking collectives: 89.3 us -> 0 us
  matrix products: 26 us -> 0 us
  local copies, waits for them, and re-layouts: 21.2 us -> 4.54 us
  between operations: 13.5 us -> 0.01 us
  other arithmetic: 12.3 us -> 0 us
  starting transfers between devices: 5.79 us -> 0 us
    pallas_call x0 -> x1, Pallas kernels: none -> 96.1 us  [local(): pl.pallas_call(functools.partial(kernel, n), out_shape=jax.ShapeDtypeStru...]
    all_to_all x1 -> x0, blocking collectives: 89.3 us -> none  [local(): lax.all_to_all(outgoing, 'expert', split_axis=0, concat_axis=0, tiled=True)]
    all_to_all x1 -> x0, waiting for transfers between devices: 82.4 us -> none  [local(): lax.all_to_all(summed.reshape(experts, capacity, model_width).astype(jnp....]
    dot_general x3 -> x0, matrix products: 26 us -> none  [the longest x1 9.48 us: local(): gate_out = jnp.dot(row_data, w_gate[0], preferred_element_type=jnp.float32)]
    all_gather x1 -> x0, waiting for transfers between devices: 17.4 us -> none  [local(): lax.all_gather(arrived, 'dp', axis=0, tiled=True).reshape(-1, model_width)]
    reduce_scatter x1 -> x0, waiting for transfers between devices: 17.2 us -> none  [local(): lax.psum_scatter(jnp.dot(hidden, w_down[0], preferred_element_type=jnp.fl...]
    gather x2 -> x0, local copies, waits for them, and re-layouts: 12.9 us -> none  [the longest x1 8.18 us: local(): gathered = per_slot[slot_index].reshape(tok_count, top_count, model_width)]
    reshape x1 -> x0, other arithmetic: 5.87 us -> none  [local(): per_slot = returned.reshape(experts * capacity, model_width)]
  transfers between devices with their start and end apart: 3 -> 0, of which waited for: 3 -> 0; matrix products, arithmetic and copies ran while one was open for 0% -> 0% of each run, Pallas kernels for 0% -> 0%
where the time goes in v1:
time: 101 us
  Pallas kernels  96.1 us (95%)
  local copies, waits for them, and re-layouts  4.54 us (4%)
    pallas_call x1, Pallas kernels, local(): pl.pallas_call(functools.partial(kernel, n), out_shape=jax.ShapeDtypeStru...  96.1 us
    unnamed x3, local copies, waits for them, and re-layouts  4.54 us

profile of v1, /device:TPU:0, one launch (start us, length us, event | category | flops | bytes accessed | tf_op | source)
XLA Modules:
  0.0 100.6 jit_solution(3687455901892046452)
XLA Ops:
  0.0 1.4 %copy.7.routes = s32[32,4]{1,0:T(8,128)} copy(s32[32,4]{0,1:T(4,128)} %param.7) | data formatting | bytes 1024 | tf_op args[1]
  1.4 1.4 %copy.8.gates = f32[32,4]{1,0:T(8,128)} copy(f32[32,4]{0,1:T(4,128)} %param.8) | data formatting | bytes 1024 | tf_op args[2]
  2.7 96.1 %shard_map.64 = bf16[32,7168]{1,0:T(8,128)(2,1)} custom-call(bf16[32,7168]{1,0:T(8,128)(2,1)} %tokens.1, s32[32,4]{1,0:T(8,128)} %copy.7.routes, f32[32,4]{1,0:T(8,128)} %copy.8.gates, bf16[1,7168,512]{2,1,0:T(8,128)(2,1)} %w_gate.1, bf16[1,7168,512]{2,1,0:T(8,128)(2,1)} %w_up.1, bf16[1,512,7168]{2,1,0:T(8,128)(2,1)} %w_down.1), custom_call_target="tpu_custom_call" | custom-call | flops 11274289152 | bytes 22020096 | tf_op jit(solution)/shard_map/pallas_call | solution.py:212
  98.8 1.8 %copy.10 = bf16[32,7168]{1,0:T(8,128)(2,1)} copy(bf16[32,7168]{1,0:T(8,128)(2,1)} %shard_map.64) | data formatting | bytes 917504

commit v2 on v1

--- a/solution.py
+++ b/solution.py
@@ -27,7 +27,7 @@
            x, mine, theirs, back, wg, wu, wd, hid,
            w_sem, fwd_send, fwd_recv, pair_send, pair_recv, sum_send, sum_recv, back_send, back_recv):
     rows, width = tokens.shape
-    top = routes.shape[1]
+    top = routes.shape[0]
     ffd = wg.shape[1]
     half, sub = n // 2, rows // 2
     expert = lax.axis_index("expert")
@@ -54,15 +54,19 @@
         pl.semaphore_signal(barrier, inc=1, device_id=device, device_id_type=MESH)
 
     x[0:rows, 0:width] = tokens[...]
-    lane = lax.broadcasted_iota(jnp.int32, (rows, LANES), 1)
-    left = jnp.zeros((rows, LANES), jnp.float32)
+    line = lax.broadcasted_iota(jnp.int32, (LANES, rows), 0)
+    left = jnp.zeros((LANES, rows), jnp.float32)
     for k in range(top):
         for part in range(3):
-            left = left + jnp.where(lane == routes[:, k:k + 1] + part * n, gates[:, k:k + 1], 0.0)
+            left = left + jnp.where(line == routes[k:k + 1, :] + part * n, gates[k:k + 1, :], 0.0)
     high = left.astype(jnp.bfloat16).astype(jnp.float32)
     mid = (left - high).astype(jnp.bfloat16).astype(jnp.float32)
     low = left - high - mid
-    x[0:rows, width:width + LANES] = jnp.where(lane < n, high, jnp.where(lane < 2 * n, mid, low)).astype(jnp.bfloat16)
+    parts = jnp.where(line < n, high, jnp.where(line < 2 * n, mid, low)).astype(jnp.bfloat16)
+    same = lax.broadcasted_iota(jnp.int32, (rows, rows), 0) == lax.broadcasted_iota(jnp.int32, (rows, rows), 1)
+    eye = jnp.where(same, 1.0, 0.0).astype(jnp.bfloat16)
+    turned = lax.dot_general(eye, parts, (((1,), (1,)), ((), ())), preferred_element_type=jnp.float32)
+    x[0:rows, width:width + LANES] = turned.astype(jnp.bfloat16)
     pl.semaphore_wait(barrier, 3)
 
     def forward(d, s, c):
@@ -70,13 +74,14 @@
         return rdma(x.at[pl.ds(a, sub)], x.at[pl.ds(b, sub)],
                     fwd_send.at[d, s, c], fwd_recv.at[d, s + 1, c], ahead[d])
 
-    def pair(b):
-        return rdma(x.at[pl.ds(b * 2 * rows, rows)], x.at[pl.ds(b * 2 * rows + rows, rows)],
-                    pair_send.at[b], pair_recv.at[b], partner)
-
-    def summed(b):
-        return rdma(x.at[pl.ds(b * 2 * rows + rows, rows), pl.ds(0, width)], theirs.at[pl.ds(b * rows, rows)],
-                    sum_send.at[b], sum_recv.at[b], partner)
+    def pair(b, c):
+        at = b * 2 * rows + c * sub
+        return rdma(x.at[pl.ds(at, sub)], x.at[pl.ds(at + rows, sub)],
+                    pair_send.at[b, c], pair_recv.at[b, c], partner)
+
+    def summed(b, c):
+        return rdma(x.at[pl.ds(b * 2 * rows + rows + c * sub, sub), pl.ds(0, width)],
+                    theirs.at[pl.ds(b * rows + c * sub, sub)], sum_send.at[b, c], sum_recv.at[b, c], partner)
 
     sent = []
 
@@ -100,7 +105,7 @@
         lane = lax.broadcasted_iota(jnp.int32, (count, LANES), 1)
         own = (lane == expert) | (lane == expert + n) | (lane == expert + 2 * n)
         weight = jnp.sum(jnp.where(own, x[span, width:width + LANES].astype(jnp.float32), 0.0), axis=1, keepdims=True)
-        wide = 512 if width % 512 == 0 else LANES
+        wide = 1792 if width % 1792 == 0 else LANES
 
         def down(j, _):
             cols = pl.ds(pl.multiple_of(j * wide, wide), wide)
@@ -113,28 +118,31 @@
             return 0
 
         lax.fori_loop(0, width // wide, down, 0)
-        for i in range(blocks):
-            start(summed(first + i))
+        for c in (0, 1):
+            for i in range(blocks):
+                start(summed(first + i, 1 - c if i == 0 else c))
 
     for c in (0, 1):
         for d in (0, 1):
             start(forward(d, 0, c))
-    start(pair(0))
+            if d == 1:
+                start(pair(0, c))
     for s in range(1, half):
         for c in (0, 1):
             for d in (0, 1):
                 forward(d, s - 1, c).wait_recv()
                 if s < half - 1 or c == d:
                     start(forward(d, s, c))
-        for d in (0, 1):
-            start(pair(slot(d, s)))
+                start(pair(slot(d, s), c))
         if s == 1:
             for load in loads:
                 load.wait()
-            pair(0).wait_recv()
+            for c in (0, 1):
+                pair(0, c).wait_recv()
             compute(0, 1)
         for d in (0, 1):
-            pair(slot(d, s)).wait_recv()
+            for c in (0, 1):
+                pair(slot(d, s), c).wait_recv()
         compute(slot(0, s), 2)
 
     def home(d, s, c):
@@ -143,51 +151,45 @@
         return rdma(from_, back.at[pl.ds((d * half + s - 1) * rows + c * sub, sub)],
                     back_send.at[d, s, c], back_recv.at[d, s - 1, c], ahead[d])
 
-    wide = 1024 if width % 1024 == 0 else LANES
+    wide = 512 if width % 512 == 0 else LANES
 
     def step(d, s, c, last):
         at = slot(1 - d, s) * rows + c * sub
+        summed(slot(1 - d, s), c).wait_recv()
         if not last:
             home(d, s + 1, c).wait_recv()
         here = (d * half + s) * rows + c * sub
 
-        def add(j, _):
-            cols = pl.ds(pl.multiple_of(j * wide, wide), wide)
+        for j in range(width // wide):
+            cols = pl.ds(j * wide, wide)
             total = mine[at:at + sub, cols].astype(jnp.float32) + theirs[at:at + sub, cols].astype(jnp.float32)
             if last:
                 mine[at:at + sub, cols] = total.astype(jnp.bfloat16)
             else:
                 total = total + back[here:here + sub, cols].astype(jnp.float32)
                 back[here:here + sub, cols] = total.astype(jnp.bfloat16)
-            return 0
-
-        lax.fori_loop(0, width // wide, add, 0)
         start(home(d, s, c))
 
     def finish(c):
+        summed(0, c).wait_recv()
         for d in (0, 1):
             home(d, 1, c).wait_recv()
         a, b, t = c * sub, half * rows + c * sub, c * sub
 
-        def add(j, _):
-            cols = pl.ds(pl.multiple_of(j * wide, wide), wide)
+        for j in range(width // wide):
+            cols = pl.ds(j * wide, wide)
             total = mine[t:t + sub, cols].astype(jnp.float32) + theirs[t:t + sub, cols].astype(jnp.float32)
             total = total + back[a:a + sub, cols].astype(jnp.float32) + back[b:b + sub, cols].astype(jnp.float32)
             out[t:t + sub, cols] = total.astype(jnp.bfloat16)
-            return 0
-
-        lax.fori_loop(0, width // wide, add, 0)
-
-    for b in range(n - 1):
-        summed(b).wait_recv()
+
     for d in (0, 1):
         step(d, half - 1, d, True)
     for d in (0, 1):
         forward(d, half - 1, d).wait_recv()
-    start(pair(n - 1))
-    pair(n - 1).wait_recv()
+        start(pair(n - 1, d))
+    for d in (0, 1):
+        pair(n - 1, d).wait_recv()
     compute(n - 1, 1)
-    summed(n - 1).wait_recv()
     for d in (0, 1):
         step(d, half, 1 - d, True)
     for i in range(1, half):
@@ -225,15 +227,15 @@
             pltpu.VMEM((4 * rows, ffd), bf),
             dma((3,)),
             dma((2, half + 1, 2)), dma((2, half + 1, 2)),
-            dma((n,)), dma((n,)),
-            dma((n,)), dma((n,)),
+            dma((n, 2)), dma((n, 2)),
+            dma((n, 2)), dma((n, 2)),
             dma((2, half + 1, 2)), dma((2, half + 1, 2)),
         ],
         compiler_params=pltpu.CompilerParams(
             collective_id=0, has_side_effects=True, vmem_limit_bytes=61 * 2 ** 20),
         cost_estimate=pl.CostEstimate(
             flops=12 * n * rows * width * ffd, bytes_accessed=6 * width * ffd, transcendentals=2 * n * rows * ffd),
-    )(tokens, routes, gate_weights, w_gate, w_up, w_down)
+    )(tokens, routes.T, gate_weights.T, w_gate, w_up, w_down)
 
 
 def solution(mesh):

time: 101 us -> 90.1 us (0.89)
  Pallas kernels: 96.1 us -> 88.1 us
  local copies, waits for them, and re-layouts: 4.54 us -> 1.82 us
    pallas_call x1, Pallas kernels: 96.1 us -> 88.1 us  [local(): pl.pallas_call(functools.partial(kernel, n), out_shape=jax.ShapeDtypeStru...]
    unnamed x3 -> x1, local copies, waits for them, and re-layouts: 4.54 us -> 1.82 us
where the time goes in v2:
time: 90.1 us; the launch traced here: 89.9 us
  Pallas kernels  88.1 us (98%)
  local copies, waits for them, and re-layouts  1.82 us (2%)
    pallas_call x1, Pallas kernels, local(): pl.pallas_call(functools.partial(kernel, n), out_shape=jax.ShapeDtypeStru...  88.1 us
    unnamed x1, local copies, waits for them, and re-layouts  1.82 us

profile of v2, /device:TPU:0, one launch (start us, length us, event | category | flops | bytes accessed | tf_op | source)
XLA Modules:
  0.0 89.9 jit_solution(12569365623400568390)
XLA Ops:
  0.0 88.1 %shard_map.64 = bf16[32,7168]{1,0:T(8,128)(2,1)} custom-call(bf16[32,7168]{1,0:T(8,128)(2,1)} %tokens.1, s32[4,32]{1,0:T(4,128)} %bitcast.2, f32[4,32]{1,0:T(4,128)} %bitcast.3, bf16[1,7168,512]{2,1,0:T(8,128)(2,1)} %w_gate.1, bf16[1,7168,512]{2,1,0:T(8,128)(2,1)} %w_up.1, bf16[1,512,7168]{2,1,0:T(8,128)(2,1)} %w_down.1), custom_call_target="tpu_custom_call" | custom-call | flops 11274289152 | bytes 22020096 | tf_op jit(solution)/shard_map/pallas_call | solution.py:214
  88.1 1.8 %copy.8 = bf16[32,7168]{1,0:T(8,128)(2,1)} copy(bf16[32,7168]{1,0:T(8,128)(2,1)} %shard_map.64) | data formatting | bytes 917504
